TPU v7x, 32 devices: a whole 2x2x4 slice. The times are simulated.
32 devices in a mesh: mem: 2 (over x), space: 16 (over z, y, core).
Axes of the slice: x: 2, y: 2, z: 4, core: 2. Of those that a mesh axis runs over, the one named last changes fastest.
Arguments:
- prior_sample_states: float32 [16, 12, 4096], P('mem', None, 'space'), may hold values from -6 to 6
- depth: float32 [4, 4096], P(None, 'space'), may hold values from 0.5 to 2
- neighbours: int32 [4, 4096], P(None, 'space'), may hold values from 0 to 767, as said below
- obs_element: int32 [16384], P('space'), may hold values from 0 to 255
- obs_count: int32 [16], P('space'), may hold values from 512 to 1024
- obs_values: float32 [16384], P('space'), may hold values from -8 to 8
- obs_error: float32 [16384], P('space'), may hold values from 0.5 to 2
Outputs:
- analysis: float32 [16, 12, 4096], P('mem', None, 'space')
Inputs may be any that keep to these rules, and one draw needn't show every extreme that they name: `neighbours`: west and south entries are e + 256 - k and east and north entries e + 256 + k for element e of its block with k from 1 to 256; the first element's west entry and the last element's east entry are at the ends.
All inputs are finite; a program needn't handle non-finite values.
Results may differ from a plain program's by a relative error of at most 0.00015.
Values sent between devices are 32-bit elements; how exact they have to be, the bound alone decides.
A program may use at most 64 MiB of HBM per device.

v0:
```python
import jax
import jax.numpy as jnp
from jax import lax
from jax.sharding import PartitionSpec as P

RIM = 256
GN_ITERS = 2


CORIOLIS = 0.5
TIME_STEP = 0.08
SECTION_DECAY = (0.0, -5.0 / 9.0, -153.0 / 128.0)
SECTION_GAIN = (1.0 / 3.0, 15.0 / 16.0, 8.0 / 15.0)
FACE_TABLE = (
    (slice(0, 2), slice(2, 4), -1.0, 0.0),
    (slice(2, 4), slice(0, 2), 1.0, 0.0),
    (slice(0, 4, 2), slice(1, 4, 2), 0.0, -1.0),
    (slice(1, 4, 2), slice(0, 4, 2), 0.0, 1.0),
)


def with_halo(cells, sides, width):
    for axis, dim in sides:
        count = lax.axis_size(axis)
        ends = count - 1
        head = lax.slice_in_dim(cells, 0, width, axis=dim)
        tail = lax.slice_in_dim(cells, cells.shape[dim] - width, cells.shape[dim], axis=dim)
        cells = jnp.concatenate(
            [
                lax.ppermute(tail, axis, [(i, (i + 1) % count) for i in range(ends)]),
                cells,
                lax.ppermute(head, axis, [((i + 1) % count, i) for i in range(ends)]),
            ],
            axis=dim,
        )
    return cells


def derive_x(values):
    diff = values[..., 2:4, :] - values[..., 0:2, :]
    return jnp.concatenate([diff, diff], axis=-2)


def derive_y(values):
    upper = values[..., 1:2, :] - values[..., 0:1, :]
    lower = values[..., 3:4, :] - values[..., 2:3, :]
    return jnp.concatenate([upper, upper, lower, lower], axis=-2)


def normal_flux(state, depth_part, normal_x, normal_y):
    return jnp.stack(
        [
            depth_part * (normal_x * state[..., 1, :, :] + normal_y * state[..., 2, :, :]),
            normal_x * state[..., 0, :, :],
            normal_y * state[..., 0, :, :],
        ],
        axis=-3,
    )


def tendency(padded, depth_padded, links, margin):
    width = links.shape[1]
    lead = padded.shape[:-2]
    fields = padded[..., margin : margin + width].reshape(lead + (3, 4, width))
    depth_own = depth_padded[:, margin : margin + width]
    height = fields[..., 0, :, :]
    flow_x = fields[..., 1, :, :]
    flow_y = fields[..., 2, :, :]
    rate_h = -(derive_x(depth_own * flow_x) + derive_y(depth_own * flow_y))
    rate_u = -derive_x(height) + CORIOLIS * flow_y
    rate_v = -derive_y(height) - CORIOLIS * flow_x
    rates = jnp.stack([rate_h, rate_u, rate_v], axis=-3)
    for face, (inner, outer, normal_x, normal_y) in enumerate(FACE_TABLE):
        beyond = jnp.take(padded, links[face], axis=-1).reshape(lead + (3, 4, width))
        depth_beyond = jnp.take(depth_padded, links[face], axis=-1)
        own = fields[..., inner, :]
        far = beyond[..., outer, :]
        depth_in = depth_own[inner]
        depth_out = depth_beyond[outer]
        speed = jnp.sqrt(jnp.maximum(depth_in, depth_out))
        jump = (
            normal_flux(own, depth_in, normal_x, normal_y)
            - normal_flux(far, depth_out, normal_x, normal_y)
            + speed * (far - own)
        )
        rates = rates.at[..., inner, :].add(jump)
    return rates.reshape(lead + (12, width))


def observe(values):
    return values[..., 0, :] + values[..., 1, :] ** 2 + values[..., 2, :] ** 2


def solve_step(hessian, vector):
    lower = jnp.linalg.cholesky(hessian)
    middle = lax.linalg.triangular_solve(lower, vector[:, None], left_side=True, lower=True)
    result = lax.linalg.triangular_solve(
        lower, middle, left_side=True, lower=True, transpose_a=True
    )
    return (result[:, 0], lower)


def mixing(weights, lower, sample_realizations):
    spread = jnp.sqrt(jnp.float32(sample_realizations - 1))
    eye = jnp.eye(sample_realizations, dtype=jnp.float32)
    inverse_t = lax.linalg.triangular_solve(
        lower, eye, left_side=True, lower=True, transpose_a=True
    )
    coef = weights[:, None] / spread + inverse_t
    return 1.0 / sample_realizations + coef - jnp.mean(coef, axis=0, keepdims=True)


def body(prior_sample_states, depth, neighbours, obs_element, obs_count, obs_values, obs_error):
    local_members = prior_sample_states.shape[0]
    sample_realizations = local_members * lax.axis_size("mem")
    slots = obs_values.shape[0]
    first_member = lax.axis_index("mem") * local_members
    depth_padded = with_halo(depth, (("space", 1),), RIM)
    state = prior_sample_states
    store = jnp.zeros_like(prior_sample_states)
    for section_index in range(3):
        padded = with_halo(state, (("space", 2),), RIM)
        store = SECTION_DECAY[section_index] * store + TIME_STEP * tendency(
            padded, depth_padded, neighbours, RIM
        )
        state = state + SECTION_GAIN[section_index] * store
    used = (jnp.arange(slots, dtype=jnp.int32) < obs_count[0]).astype(jnp.float32)
    weight = used / obs_error
    probed_readings = jnp.take(state, obs_element, axis=2).reshape(local_members, 3, 4, slots)
    means = jnp.mean(probed_readings, axis=2)
    zbar = lax.psum(jnp.sum(means, axis=0), "mem") / sample_realizations
    spread_z = (means - zbar) / jnp.sqrt(jnp.float32(sample_realizations - 1))
    weights = jnp.zeros((sample_realizations,), jnp.float32)
    eye = jnp.eye(sample_realizations, dtype=jnp.float32)
    lower = eye
    for iteration in range(GN_ITERS):
        if iteration == 0:
            centre = zbar
        else:
            own_weights = lax.dynamic_slice_in_dim(weights, first_member, local_members)
            partial_shift = jnp.einsum(
                "m,mco->co", own_weights, spread_z, precision=lax.Precision.HIGHEST
            )
            centre = zbar + lax.psum(partial_shift, "mem")
        centre_obs = observe(centre)
        sens = (observe(centre[None] + spread_z) - centre_obs[None]) * weight[None]
        innov = (obs_values - centre_obs) * weight
        share = slots // lax.axis_size("mem")
        regrouped = lax.all_to_all(sens, "mem", split_axis=1, concat_axis=0, tiled=True)
        innov_part = lax.dynamic_slice_in_dim(innov, lax.axis_index("mem") * share, share)
        gram, pulled = lax.psum(
            (
                jnp.dot(regrouped, regrouped.T, precision=lax.Precision.HIGHEST),
                jnp.dot(regrouped, innov_part, precision=lax.Precision.HIGHEST),
            ),
            ("mem", "space"),
        )
        hessian = eye + gram
        grad = weights - pulled
        step_vec, lower = solve_step(hessian, grad)
        weights = weights - step_vec
    combination_coefficients = mixing(weights, lower, sample_realizations)
    mixed = jnp.einsum(
        "mn,mke->nke",
        combination_coefficients,
        lax.all_to_all(state, "mem", split_axis=2, concat_axis=0, tiled=True),
        precision=lax.Precision.HIGHEST,
    )
    return lax.all_to_all(mixed, "mem", split_axis=0, concat_axis=2, tiled=True)


def solution(mesh):
    placed = (
        P("mem", None, "space"),
        P(None, "space"),
        P(None, "space"),
        P("space"),
        P("space"),
        P("space"),
        P("space"),
    )
    return jax.shard_map(
        body, mesh=mesh, in_specs=placed, out_specs=P("mem", None, "space"), check_vma=False
    )
```

profile of v0, /device:TPU:0, one launch (start us, length us, event | category | flops | bytes accessed | tf_op | source)
XLA Modules:
  0.0 283.8 jit_solution(11385411563992114289)
XLA Ops:
  1.3 3.0 %collective-permute-start.2 = (f32[8,12,256]{2,0,1:T(8,128)}, f32[8,12,256]{2,0,1:T(8,128)S(1)}, u32[]{:S(2)}, u32[]{:S(2)}) collective-permute-start(f32[8,12,256]{2,0,1:T(8,128)} %param.28), channel_id=1, source_target_pairs={{0,1},{1,2},{2,3},{3,4},{4,5},{5,6},{6,7},{7,8},{8,9},{9,10},{10,1... | collective-permute-start | bytes 294920 | tf_op jit(solution)/shard_map/ppermute | solution.py:30
  4.3 1.3 collective-permute-start.1
  5.6 5.1 %collective-permute-start = (f32[4,256]{1,0:T(4,128)}, f32[4,256]{1,0:T(4,128)S(1)}, u32[]{:S(2)}, u32[]{:S(2)}) collective-permute-start(f32[4,256]{1,0:T(4,128)} %param.29), channel_id=1, source_target_pairs={{0,1},{1,2},{2,3},{3,4},{4,5},{5,6},{6,7},{7,8},{8,9},{9,10},{10,1... | collective-permute-start | bytes 12296 | tf_op jit(solution)/shard_map/ppermute | solution.py:30
  23.7 1.4 maximum_sqrt_fusion.2
  25.0 1.4 fusion.108
  27.7 1.6 pad_maximum_fusion
  29.3 2.2 copy.393
  31.5 2.0 gather_fusion.2
  33.5 2.0 gather_fusion.4
  35.5 2.1 gather_fusion.8
  37.6 2.0 gather_fusion.6
  39.6 1.6 select_bitcast_fusion.11
  41.7 1.6 select_bitcast_fusion.10
  45.7 1.4 fusion.164
  53.0 1.3 collective-permute-start.5
  54.3 4.5 %collective-permute-start.4 = (f32[8,12,256]{2,0,1:T(8,128)S(1)}, f32[8,12,256]{2,0,1:T(8,128)S(1)}, u32[]{:S(2)}, u32[]{:S(2)}) collective-permute-start(f32[8,12,256]{2,0,1:T(8,128)S(1)} %bitcast_add_fusion.2), channel_id=1, source_target_pairs={{0,1},{1,2},{2,3},{3,4},{4,5},{5,6},{6,7},{7,8},{8,9},{9,10},{10,1... | collective-permute-start | bytes 294920 | tf_op jit(solution)/shard_map/ppermute | solution.py:30
  60.2 2.2 copy.409
  62.4 2.1 gather_fusion.9
  64.6 2.1 gather_fusion.10
  66.7 2.2 gather_fusion.12
  68.9 2.1 gather_fusion.11
  71.0 1.6 select_bitcast_fusion.7
  78.0 1.4 fusion.163
  86.6 1.3 collective-permute-start.7
  87.9 5.2 %collective-permute-start.6 = (f32[8,12,256]{2,0,1:T(8,128)S(1)}, f32[8,12,256]{2,0,1:T(8,128)S(1)}, u32[]{:S(2)}, u32[]{:S(2)}) collective-permute-start(f32[8,12,256]{2,0,1:T(8,128)S(1)} %bitcast_add_fusion.1), channel_id=1, source_target_pairs={{0,1},{1,2},{2,3},{3,4},{4,5},{5,6},{6,7},{7,8},{8,9},{9,10},{10,1... | collective-permute-start | bytes 294920 | tf_op jit(solution)/shard_map/ppermute | solution.py:30
  94.6 2.2 copy.419
  96.8 2.1 gather_fusion.13
  98.9 2.1 gather_fusion.14
  101.1 2.1 gather_fusion.16
  103.2 2.2 gather_fusion.15
  105.4 1.6 select_bitcast_fusion.3
  108.1 1.4 fusion.78
  113.2 1.4 fusion.162
  124.2 9.1 %gather_fusion = f32[1024,8,12]{2,1,0:T(8,128)} fusion(f32[8,12,256]{1,0,2:T(8,128)S(1)} %copy.429, s32[1024]{0:T(1024)S(1)} %copy-done.33), kind=kCustom, calls=%fused_computation.16 | custom fusion | bytes 790528 | tf_op jit(solution)/shard_map/jit(_take)/gather | solution.py:129
  133.2 2.9 %copy.430 = f32[8,12,1024]{2,0,1:T(8,128)S(1)} copy(f32[8,12,1024]{1,0,2:T(8,128)} %bitcast.287) | data formatting | bytes 786432 | tf_op jit(solution)/shard_map/jit(_take)/gather | solution.py:129
  136.2 8.2 %psum.42 = f32[3,1024]{1,0:T(4,128)S(1)} all-reduce(f32[3,1024]{1,0:T(4,128)S(1)} %multiply_reduce_fusion), channel_id=1, replica_groups=mesh['mem'=2,'space'=16] {'mem'}, use_global_device_ids=true, to_apply=%region_8.11 | all-reduce | flops 3072 | bytes 24576 | tf_op jit(solution)/shard_map/psum | solution.py:131
  146.3 3.3 %all-to-all-start = ((f32[8,2,512]{2,0,1:T(8,128)}), f32[8,2,512]{2,0,1:T(8,128)S(1)}, u32[]{:S(2)}, u32[]{:S(2)}) async-start(f32[8,2,512]{2,0,1:T(8,128)} %copy.431), calls=%async_computation | async-start | bytes 65536 | tf_op jit(solution)/shard_map/all_to_all | solution.py:149
  149.5 1.6 reshape.1204
  151.2 2.3 all-to-all-done
  153.8 47.9 %all-reduce.1 = (f32[16,16]{0,1:T(8,128)S(1)}, f32[16]{0:T(128)S(1)}) all-reduce(f32[16,16]{0,1:T(8,128)S(1)} %fusion.65, f32[16]{0:T(128)S(1)} %convolution_bitcast_fusion.1), channel_id=1, replica_groups=mesh['mem'=2,'space'=16] {'mem','space'}, use_global_device_ids=true, to_apply=%region_9.12 | all-reduce | flops 272 | bytes 2176 | tf_op jit(solution)/shard_map/psum | solution.py:151
  201.8 1.5 cholesky.44
  206.4 8.9 %psum.45 = f32[3,1024]{1,0:T(4,128)S(1)} all-reduce(f32[3,1024]{1,0:T(4,128)S(1)} %bitcast.319), channel_id=1, replica_groups=mesh['mem'=2,'space'=16] {'mem'}, use_global_device_ids=true, to_apply=%region_13.19 | all-reduce | flops 3072 | bytes 24576 | tf_op jit(solution)/shard_map/psum | solution.py:144
  216.7 3.3 %all-to-all-start.1 = ((f32[8,2,512]{2,0,1:T(8,128)}), f32[8,2,512]{2,0,1:T(8,128)S(1)}, u32[]{:S(2)}, u32[]{:S(2)}) async-start(f32[8,2,512]{2,0,1:T(8,128)} %copy.434), calls=%async_computation.1 | async-start | bytes 65536 | tf_op jit(solution)/shard_map/all_to_all | solution.py:149
  220.1 3.8 %all-to-all-done.1 = f32[8,2,512]{2,0,1:T(8,128)S(1)} async-done(((f32[8,2,512]{2,0,1:T(8,128)}), f32[8,2,512]{2,0,1:T(8,128)S(1)}, u32[]{:S(2)}, u32[]{:S(2)}) %all-to-all-start.1) | async-done | bytes 32800 | tf_op jit(solution)/shard_map/all_to_all | solution.py:149
  223.9 3.3 %all-to-all-start.2 = ((f32[2,1,12288]{2,1,0:T(1,128)}), f32[2,1,12288]{2,1,0:T(1,128)S(1)}, u32[]{:S(2)}, u32[]{:S(2)}) async-start(f32[2,1,12288]{2,1,0:T(1,128)} %reshape.1204), calls=%async_computation.2 | async-start | bytes 196608 | tf_op jit(solution)/shard_map/all_to_all | solution.py:166
  227.6 39.8 %all-reduce = (f32[16,16]{0,1:T(8,128)S(1)}, f32[16]{0:T(128)S(1)}) all-reduce(f32[16,16]{0,1:T(8,128)S(1)} %fusion.62, f32[16]{0:T(128)S(1)} %convolution_bitcast_fusion), channel_id=1, replica_groups=mesh['mem'=2,'space'=16] {'mem','space'}, use_global_device_ids=true, to_apply=%region_14.20 | all-reduce | flops 272 | bytes 2176 | tf_op jit(solution)/shard_map/psum | solution.py:151
  267.4 1.5 cholesky.55
  275.3 7.8 %all_to_all.68 = f32[16,12,128]{2,1,0:T(8,128)S(1)} all-to-all(f32[16,12,128]{2,1,0:T(8,128)S(1)} %copy.440), channel_id=1, replica_groups=mesh['mem'=2,'space'=16] {'mem'}, dimensions={0} | all-to-all | bytes 196608 | tf_op jit(solution)/shard_map/all_to_all | solution.py:169
  (306 shorter events, 66.5 us)
Async XLA Ops:
  0.0 27.7 %collective-permute-start.3 = (f32[8,12,256]{2,0,1:T(8,128)}, f32[8,12,256]{2,0,1:T(8,128)S(1)}, u32[]{:S(2)}, u32[]{:S(2)}) collective-permute-start(f32[8,12,256]{2,0,1:T(8,128)} %param.28), channel_id=1, source_target_pairs={{1,0},{2,1},{3,2},{4,3},{5,4},{6,5},{7,6},{8,7},{9,8},{10,9},{11,1... | collective-permute-start | bytes 294920 | tf_op jit(solution)/shard_map/ppermute | solution.py:32
  1.3 26.4 %collective-permute-start.2 = (f32[8,12,256]{2,0,1:T(8,128)}, f32[8,12,256]{2,0,1:T(8,128)S(1)}, u32[]{:S(2)}, u32[]{:S(2)}) collective-permute-start(f32[8,12,256]{2,0,1:T(8,128)} %param.28), channel_id=1, source_target_pairs={{0,1},{1,2},{2,3},{3,4},{4,5},{5,6},{6,7},{7,8},{8,9},{9,10},{10,1... | collective-permute-start | bytes 294920 | tf_op jit(solution)/shard_map/ppermute | solution.py:30
  4.3 15.0 %collective-permute-start.1 = (f32[4,256]{1,0:T(4,128)}, f32[4,256]{1,0:T(4,128)S(1)}, u32[]{:S(2)}, u32[]{:S(2)}) collective-permute-start(f32[4,256]{1,0:T(4,128)} %param.29), channel_id=1, source_target_pairs={{1,0},{2,1},{3,2},{4,3},{5,4},{6,5},{7,6},{8,7},{9,8},{10,9},{11,1... | collective-permute-start | bytes 12296 | tf_op jit(solution)/shard_map/ppermute | solution.py:32
  5.6 13.8 %collective-permute-start = (f32[4,256]{1,0:T(4,128)}, f32[4,256]{1,0:T(4,128)S(1)}, u32[]{:S(2)}, u32[]{:S(2)}) collective-permute-start(f32[4,256]{1,0:T(4,128)} %param.29), channel_id=1, source_target_pairs={{0,1},{1,2},{2,3},{3,4},{4,5},{5,6},{6,7},{7,8},{8,9},{9,10},{10,1... | collective-permute-start | bytes 12296 | tf_op jit(solution)/shard_map/ppermute | solution.py:30
  13.2 26.4 %copy-start.42 = (pred[256]{0:T(512)(128)(4,1)}, pred[256]{0:T(512)(128)(4,1)S(1)}, u32[]{:S(2)}) copy-start(pred[256]{0:T(512)(128)(4,1)S(1)} %get-tuple-element.222) | copy-start | bytes 772
  13.2 28.4 %copy-start.41 = (pred[256]{0:T(512)(128)(4,1)}, pred[256]{0:T(512)(128)(4,1)S(1)}, u32[]{:S(2)}) copy-start(pred[256]{0:T(512)(128)(4,1)S(1)} %get-tuple-element.221) | copy-start | bytes 772
  13.2 14.4 %copy-start.39 = (pred[256]{0:T(512)(128)(4,1)}, pred[256]{0:T(512)(128)(4,1)S(1)}, u32[]{:S(2)}) copy-start(pred[256]{0:T(512)(128)(4,1)S(1)} %get-tuple-element.220) | copy-start | bytes 772
  13.3 14.4 %copy-start.40 = (pred[256]{0:T(512)(128)(4,1)}, pred[256]{0:T(512)(128)(4,1)S(1)}, u32[]{:S(2)}) copy-start(pred[256]{0:T(512)(128)(4,1)S(1)} %get-tuple-element.219) | copy-start | bytes 772
  15.8 19.7 %copy-start.34 = (s32[1024]{0:T(1024)}, s32[1024]{0:T(1024)S(1)}, u32[]{:S(2)}) copy-start(s32[1024]{0:T(1024)S(1)} %pad_clamp_fusion.3) | copy-start | bytes 12292
  15.8 19.7 %copy-start.35 = (s32[1024]{0:T(1024)}, s32[1024]{0:T(1024)S(1)}, u32[]{:S(2)}) copy-start(s32[1024]{0:T(1024)S(1)} %pad_clamp_fusion.2) | copy-start | bytes 12292
  15.9 19.7 %copy-start.36 = (s32[1024]{0:T(1024)}, s32[1024]{0:T(1024)S(1)}, u32[]{:S(2)}) copy-start(s32[1024]{0:T(1024)S(1)} %pad_clamp_fusion) | copy-start | bytes 12292
  15.9 21.7 %copy-start.37 = (s32[1024]{0:T(1024)}, s32[1024]{0:T(1024)S(1)}, u32[]{:S(2)}) copy-start(s32[1024]{0:T(1024)S(1)} %pad_clamp_fusion.1) | copy-start | bytes 12292
  18.0 19.6 %copy-start.20 = (f32[2,256]{1,0:T(2,128)}, f32[2,256]{1,0:T(2,128)S(1)}, u32[]{:S(2)}) copy-start(f32[2,256]{1,0:T(2,128)S(1)} %slice.827) | copy-start | bytes 6148
  18.7 18.9 %copy-start.18 = (f32[2,256]{1,0:T(2,128)}, f32[2,256]{1,0:T(2,128)S(1)}, u32[]{:S(2)}) copy-start(f32[2,256]{1,0:T(2,128)S(1)} %slice.816) | copy-start | bytes 6148
  22.8 14.8 %copy-start.24 = (f32[2,256]{1,0:T(2,128)}, f32[2,256]{1,0:T(2,128)S(1)}, u32[]{:S(2)}) copy-start(f32[2,256]{1,0:T(2,128)S(1)} %slice.833) | copy-start | bytes 6148
  23.6 14.0 %copy-start.22 = (f32[2,256]{1,0:T(2,128)}, f32[2,256]{1,0:T(2,128)S(1)}, u32[]{:S(2)}) copy-start(f32[2,256]{1,0:T(2,128)S(1)} %slice.822) | copy-start | bytes 6148
  25.0 12.6 %copy-start.27 = (f32[2,256]{1,0:T(2,128)}, f32[2,256]{1,0:T(2,128)S(1)}, u32[]{:S(2)}) copy-start(f32[2,256]{1,0:T(2,128)S(1)} %get-tuple-element.210) | copy-start | bytes 6148
  25.0 12.6 %copy-start.30 = (f32[2,256]{1,0:T(2,128)}, f32[2,256]{1,0:T(2,128)S(1)}, u32[]{:S(2)}) copy-start(f32[2,256]{1,0:T(2,128)S(1)} %get-tuple-element.211) | copy-start | bytes 6148
  39.6 5.3 %copy-start = (f32[8,12,256]{2,0,1:T(8,128)S(1)}, f32[8,12,256]{2,0,1:T(8,128)}, u32[]{:S(2)}) copy-start(f32[8,12,256]{2,0,1:T(8,128)} %param.28) | copy-start | bytes 294916
  41.2 6.6 %copy-start.5 = (f32[256,8,12]{2,1,0:T(8,128)S(1)}, f32[256,8,12]{2,1,0:T(8,128)}, u32[]{:S(2)}) copy-start(f32[256,8,12]{2,1,0:T(8,128)} %gather_fusion.8) | copy-start | bytes 294916
  43.2 6.1 %copy-start.2 = (f32[256,8,12]{2,1,0:T(8,128)S(1)}, f32[256,8,12]{2,1,0:T(8,128)}, u32[]{:S(2)}) copy-start(f32[256,8,12]{2,1,0:T(8,128)} %gather_fusion.6) | copy-start | bytes 294916
  49.2 9.5 %copy-start.28 = (f32[2,256]{1,0:T(2,128)S(1)}, f32[2,256]{1,0:T(2,128)}, u32[]{:S(2)}) copy-start(f32[2,256]{1,0:T(2,128)} %copy-done.27) | copy-start | bytes 6148
  49.2 9.5 %copy-start.31 = (f32[2,256]{1,0:T(2,128)S(1)}, f32[2,256]{1,0:T(2,128)}, u32[]{:S(2)}) copy-start(f32[2,256]{1,0:T(2,128)} %copy-done.30) | copy-start | bytes 6148
  52.9 18.2 %copy-start.43 = (pred[256]{0:T(512)(128)(4,1)S(1)}, pred[256]{0:T(512)(128)(4,1)}, u32[]{:S(2)}) copy-start(pred[256]{0:T(512)(128)(4,1)} %copy-done.42) | copy-start | bytes 772
  53.0 6.5 %collective-permute-start.5 = (f32[8,12,256]{2,0,1:T(8,128)S(1)}, f32[8,12,256]{2,0,1:T(8,128)S(1)}, u32[]{:S(2)}, u32[]{:S(2)}) collective-permute-start(f32[8,12,256]{2,0,1:T(8,128)S(1)} %bitcast_add_fusion.2), channel_id=1, source_target_pairs={{1,0},{2,1},{3,2},{4,3},{5,4},{6,5},{7,6},{8,7},{9,8},{10,9},{11,1... | collective-permute-start | bytes 294920 | tf_op jit(solution)/shard_map/ppermute | solution.py:32
  54.3 5.2 %collective-permute-start.4 = (f32[8,12,256]{2,0,1:T(8,128)S(1)}, f32[8,12,256]{2,0,1:T(8,128)S(1)}, u32[]{:S(2)}, u32[]{:S(2)}) collective-permute-start(f32[8,12,256]{2,0,1:T(8,128)S(1)} %bitcast_add_fusion.2), channel_id=1, source_target_pairs={{0,1},{1,2},{2,3},{3,4},{4,5},{5,6},{6,7},{7,8},{8,9},{9,10},{10,1... | collective-permute-start | bytes 294920 | tf_op jit(solution)/shard_map/ppermute | solution.py:30
  72.7 6.8 %copy-start.21 = (f32[2,256]{1,0:T(2,128)S(1)}, f32[2,256]{1,0:T(2,128)}, u32[]{:S(2)}) copy-start(f32[2,256]{1,0:T(2,128)} %copy-done.20) | copy-start | bytes 6148
  72.7 7.4 %copy-start.6 = (f32[256,8,12]{2,1,0:T(8,128)S(1)}, f32[256,8,12]{2,1,0:T(8,128)}, u32[]{:S(2)}) copy-start(f32[256,8,12]{2,1,0:T(8,128)} %gather_fusion.12) | copy-start | bytes 294916
  75.4 6.8 %copy-start.4 = (f32[256,8,12]{2,1,0:T(8,128)S(1)}, f32[256,8,12]{2,1,0:T(8,128)}, u32[]{:S(2)}) copy-start(f32[256,8,12]{2,1,0:T(8,128)} %gather_fusion.11) | copy-start | bytes 294916
  80.1 4.3 %copy-start.26 = (f32[2,256]{1,0:T(2,128)S(1)}, f32[2,256]{1,0:T(2,128)}, u32[]{:S(2)}) copy-start(f32[2,256]{1,0:T(2,128)} %maximum_sqrt_fusion) | copy-start | bytes 6148
  81.5 4.4 %copy-start.45 = (s32[2]{0:T(128)S(1)}, s32[2]{0:T(128)}, u32[]{:S(2)}) copy-start(s32[2]{0:T(128)} %get-tuple-element.223) | copy-start | bytes 28
  81.5 11.6 %copy-start.29 = (f32[2,256]{1,0:T(2,128)S(1)}, f32[2,256]{1,0:T(2,128)}, u32[]{:S(2)}) copy-start(f32[2,256]{1,0:T(2,128)} %copy-done.27) | copy-start | bytes 6148
  81.5 11.6 %copy-start.32 = (f32[2,256]{1,0:T(2,128)S(1)}, f32[2,256]{1,0:T(2,128)}, u32[]{:S(2)}) copy-start(f32[2,256]{1,0:T(2,128)} %copy-done.30) | copy-start | bytes 6148
  86.6 7.2 %collective-permute-start.7 = (f32[8,12,256]{2,0,1:T(8,128)S(1)}, f32[8,12,256]{2,0,1:T(8,128)S(1)}, u32[]{:S(2)}, u32[]{:S(2)}) collective-permute-start(f32[8,12,256]{2,0,1:T(8,128)S(1)} %bitcast_add_fusion.1), channel_id=1, source_target_pairs={{1,0},{2,1},{3,2},{4,3},{5,4},{6,5},{7,6},{8,7},{9,8},{10,9},{11,1... | collective-permute-start | bytes 294920 | tf_op jit(solution)/shard_map/ppermute | solution.py:32
  87.9 5.9 %collective-permute-start.6 = (f32[8,12,256]{2,0,1:T(8,128)S(1)}, f32[8,12,256]{2,0,1:T(8,128)S(1)}, u32[]{:S(2)}, u32[]{:S(2)}) collective-permute-start(f32[8,12,256]{2,0,1:T(8,128)S(1)} %bitcast_add_fusion.1), channel_id=1, source_target_pairs={{0,1},{1,2},{2,3},{3,4},{4,5},{5,6},{6,7},{7,8},{8,9},{9,10},{10,1... | collective-permute-start | bytes 294920 | tf_op jit(solution)/shard_map/ppermute | solution.py:30
  107.1 8.8 %copy-start.3 = (f32[256,8,12]{2,1,0:T(8,128)S(1)}, f32[256,8,12]{2,1,0:T(8,128)}, u32[]{:S(2)}) copy-start(f32[256,8,12]{2,1,0:T(8,128)} %gather_fusion.16) | copy-start | bytes 294916
  110.5 8.1 %copy-start.1 = (f32[256,8,12]{2,1,0:T(8,128)S(1)}, f32[256,8,12]{2,1,0:T(8,128)}, u32[]{:S(2)}) copy-start(f32[256,8,12]{2,1,0:T(8,128)} %gather_fusion.15) | copy-start | bytes 294916
  117.3 4.2 %copy-start.13 = (f32[8,1,2,256]{3,0,2,1:T(8,128)S(1)}, f32[8,1,2,256]{3,0,2,1:T(8,128)}, u32[]{:S(2)}) copy-start(f32[8,1,2,256]{3,0,2,1:T(8,128)} %get-tuple-element.159) | copy-start | bytes 49156
  117.3 4.2 %copy-start.14 = (f32[8,1,2,256]{3,0,2,1:T(8,128)S(1)}, f32[8,1,2,256]{3,0,2,1:T(8,128)}, u32[]{:S(2)}) copy-start(f32[8,1,2,256]{3,0,2,1:T(8,128)} %get-tuple-element.160) | copy-start | bytes 49156
  117.3 5.0 %copy-start.49 = (s32[2]{0:T(128)S(1)}, s32[2]{0:T(128)}, u32[]{:S(2)}) copy-start(s32[2]{0:T(128)} %get-tuple-element.224) | copy-start | bytes 28
  117.3 5.7 %copy-start.46 = (s32[2]{0:T(128)S(1)}, s32[2]{0:T(128)}, u32[]{:S(2)}) copy-start(s32[2]{0:T(128)} %get-tuple-element.223) | copy-start | bytes 28
  118.6 5.6 %copy-start.33 = (s32[1024]{0:T(1024)S(1)}, s32[1024]{0:T(1024)}, u32[]{:S(2)}) copy-start(s32[1024]{0:T(1024)} %fusion.145) | copy-start | bytes 12292
  123.7 12.5 %copy-start.50 = (pred[1024]{0:T(1024)(128)(4,1)S(1)}, pred[1024]{0:T(1024)(128)(4,1)}, u32[]{:S(2)}) copy-start(pred[1024]{0:T(1024)(128)(4,1)} %compare_and_fusion) | copy-start | bytes 3076
  124.2 21.4 %copy-start.38 = (f32[1024]{0:T(1024)S(1)}, f32[1024]{0:T(1024)}, u32[]{:S(2)}) copy-start(f32[1024]{0:T(1024)} %param.33) | copy-start | bytes 12292
  124.2 21.4 %copy-start.51 = (f32[1024]{0:T(1024)S(1)}, f32[1024]{0:T(1024)}, u32[]{:S(2)}) copy-start(f32[1024]{0:T(1024)} %param.34) | copy-start | bytes 12292
  146.3 7.2 %all-to-all-start = ((f32[8,2,512]{2,0,1:T(8,128)}), f32[8,2,512]{2,0,1:T(8,128)S(1)}, u32[]{:S(2)}, u32[]{:S(2)}) async-start(f32[8,2,512]{2,0,1:T(8,128)} %copy.431), calls=%async_computation | async-start | bytes 65536 | tf_op jit(solution)/shard_map/all_to_all | solution.py:149
  216.7 7.2 %all-to-all-start.1 = ((f32[8,2,512]{2,0,1:T(8,128)}), f32[8,2,512]{2,0,1:T(8,128)S(1)}, u32[]{:S(2)}, u32[]{:S(2)}) async-start(f32[8,2,512]{2,0,1:T(8,128)} %copy.434), calls=%async_computation.1 | async-start | bytes 65536 | tf_op jit(solution)/shard_map/all_to_all | solution.py:149
  223.9 48.0 %all-to-all-start.2 = ((f32[2,1,12288]{2,1,0:T(1,128)}), f32[2,1,12288]{2,1,0:T(1,128)S(1)}, u32[]{:S(2)}, u32[]{:S(2)}) async-start(f32[2,1,12288]{2,1,0:T(1,128)} %reshape.1204), calls=%async_computation.2 | async-start | bytes 196608 | tf_op jit(solution)/shard_map/all_to_all | solution.py:166
  (15 other events, 44.0 us)
where the time goes:
time: 286 us; the launch traced here: 284 us
  blocking collectives  113 us (40%)
  local copies, waits for them, and re-layouts  64.6 us (23%)
  other arithmetic  63.3 us (22%)
  starting transfers between devices  32.8 us (11%)
  waiting for transfers between devices  6.11 us (2%)
    psum x2, blocking collectives, body(): lax.psum((jnp.dot(regrouped, regrouped.T, precision=lax.Precision.HIGHEST...  87.7 us
    gather x12, local copies, waits for them, and re-layouts, tendency(): jnp.take(padded, links[face], axis=-1).reshape(lead + (3, 4, width))  25.2 us
    ppermute x4, starting transfers between devices, with_halo(): lax.ppermute(tail, axis, [(i, (i + 1) % count) for i in range(ends)])  17.8 us
    mul x21, other arithmetic, normal_flux(): depth_part * (normal_x * state[..., 1, :, :] + normal_y * state[..., 2, :...  14.5 us
    select_n x12, other arithmetic, tendency(): jnp.take(padded, links[face], axis=-1).reshape(lead + (3, 4, width))  14.3 us
    gather x2, local copies, waits for them, and re-layouts, body(): jnp.take(state, obs_element, axis=2).reshape(local_members, 3, 4, slots)  12 us
    psum x1, blocking collectives, body(): centre = zbar + lax.psum(partial_shift, 'mem')  8.94 us
    psum x1, blocking collectives, body(): zbar = lax.psum(jnp.sum(means, axis=0), 'mem') / sample_realizations  8.16 us
  transfers between devices with their start and end apart: 11, of which 2 were waited for; matrix products, arithmetic and copies ran while one was open for 8% of the time, Pallas kernels for 0%

commit v1 on v0

v1 whole, which is shorter than its diff:
```python
import functools
import math

import jax
import jax.numpy as jnp
from jax import lax
from jax.experimental import pallas as pl
from jax.experimental.pallas import tpu as pltpu
from jax.sharding import PartitionSpec as P

GN_ITERS = 2
CORIOLIS = 0.5
TIME_STEP = 0.08
SECTION_DECAY = (0.0, -5.0 / 9.0, -153.0 / 128.0)
SECTION_GAIN = (1.0 / 3.0, 15.0 / 16.0, 8.0 / 15.0)
FACES = (
    ((0, 1), (2, 3), -1.0, 0.0, 0),
    ((2, 3), (0, 1), 1.0, 0.0, 1),
    ((0, 2), (1, 3), 0.0, -1.0, 0),
    ((1, 3), (0, 2), 0.0, 1.0, 1),
)
SENT = ((1, 2, 3), (0, 1, 2))
MESH = pl.DeviceIdType.MESH
F32, BF16 = jnp.float32, jnp.bfloat16


def split(x):
    high = x.astype(BF16)
    rest = x - high.astype(F32)
    middle = rest.astype(BF16)
    low = (rest - middle.astype(F32)).astype(BF16)
    return jnp.concatenate([high, middle, low], axis=0)


def pick(x, one_hot):
    rows = x.shape[0]
    y = jnp.dot(split(x), one_hot, preferred_element_type=F32)
    return y[:rows] + y[rows : 2 * rows] + y[2 * rows :]


def kernel(
    nm, ns,
    x_ref, dep_ref, nb_ref, oe_ref, cnt_ref, ov_ref, er_ref,
    out_ref,
    st, store, halo, dhalo, oh, fc, em, parts, sums,
    h_send, h_recv, d_send, d_recv, e_send, e_recv, f_send, f_recv, s_send, s_recv,
):
    mm, me = lax.axis_index("mem"), lax.axis_index("space")
    lm, _, width = x_ref.shape
    members = nm * lm
    space_peers = [(mm, lax.rem(me + d, ns)) for d in range(1, ns)]
    mem_peers = [(lax.rem(mm + d, nm), me) for d in range(1, nm)]

    barrier = pltpu.get_barrier_semaphore()
    for peer in space_peers + mem_peers:
        pl.semaphore_signal(barrier, inc=1, device_id=peer, device_id_type=MESH)

    for n in range(4):
        for f in range(3):
            st[0, n * 3 + f] = x_ref[:, f * 4 + n, :]
    has = (me > 0, me < ns - 1)
    for side in range(2):

        @pl.when(jnp.logical_not(has[side]))
        def _():
            for s in range(3):
                halo[s, side] = jnp.zeros(halo.shape[2:], F32)
            dhalo[side] = jnp.zeros(dhalo.shape[1:], F32)

    pl.semaphore_wait(barrier, len(space_peers) + len(mem_peers))

    def halo_copy(s, side):
        first = SENT[1 - side][0] * 3
        target = (mm, lax.rem(me + (ns - 1 if side == 0 else 1), ns))
        return pltpu.make_async_remote_copy(
            src_ref=st.at[s, pl.ds(first, 9)],
            dst_ref=halo.at[s, 1 - side],
            send_sem=h_send.at[s, 1 - side],
            recv_sem=h_recv.at[s, 1 - side],
            device_id=target,
            device_id_type=MESH,
        )

    def depth_copy(side):
        target = (mm, lax.rem(me + (ns - 1 if side == 0 else 1), ns))
        return pltpu.make_async_remote_copy(
            src_ref=dep_ref,
            dst_ref=dhalo.at[1 - side],
            send_sem=d_send.at[1 - side],
            recv_sem=d_recv.at[1 - side],
            device_id=target,
            device_id_type=MESH,
        )

    def send_halo(s):
        for side in range(2):

            @pl.when(has[side])
            def _():
                halo_copy(s, side).start()

    for side in range(2):

        @pl.when(has[side])
        def _():
            depth_copy(side).start()

    send_halo(0)

    rows = lax.broadcasted_iota(jnp.int32, (width, width), 0)
    for face in range(4):
        side = FACES[face][4]
        link = nb_ref[face : face + 1, :]
        oh[face, 0] = jnp.where(rows + width == link, 1.0, 0.0).astype(BF16)
        oh[face, 1] = jnp.where(rows + 2 * width * side == link, 1.0, 0.0).astype(BF16)

    slots = ov_ref.shape[1]
    slot = lax.broadcasted_iota(jnp.int32, (1, slots), 1)
    weight = jnp.where(slot < cnt_ref[0], 1.0, 0.0) / er_ref[...]
    square = weight * weight
    both = jnp.concatenate(
        [jnp.broadcast_to(square, (8, slots)), jnp.broadcast_to(square * ov_ref[...], (8, slots))],
        axis=0,
    )
    at = jnp.where(
        lax.broadcasted_iota(jnp.int32, (width, slots), 0) == oe_ref[...], 1.0, 0.0
    ).astype(BF16)
    y = lax.dot_general(split(both), at, (((1,), (1,)), ((), ())), preferred_element_type=F32)
    y = y[:16] + y[16:32] + y[32:]
    w2, wo = y[0:1], y[8:9]

    def tall(ref, n):
        return jnp.broadcast_to(ref[n : n + 1, :], (lm, width))

    own_depth = [tall(dep_ref, n) for n in range(4)]
    depth_out, speed = {}, {}

    for s in range(3):
        q = [[st[s, n * 3 + f] for f in range(3)] for n in range(4)]
        near = []
        for face, (_, outer, _, _, side) in enumerate(FACES):
            x = jnp.concatenate([q[n][f] for n in outer for f in range(3)], axis=0)
            near.append(pick(x, oh[face, 0]))
        hu = [own_depth[n] * q[n][1] for n in range(4)]
        hv = [own_depth[n] * q[n][2] for n in range(4)]
        rate = [[None] * 3 for _ in range(4)]
        for n in range(4):
            b, a2 = n % 2, n - n % 2
            rate[n][0] = -((hu[2 + b] - hu[b]) + (hv[a2 + 1] - hv[a2]))
            rate[n][1] = q[b][0] - q[2 + b][0] + CORIOLIS * q[n][2]
            rate[n][2] = q[a2][0] - q[a2 + 1][0] - CORIOLIS * q[n][1]
        if s == 0:
            for side in range(2):

                @pl.when(has[side])
                def _():
                    depth_copy(1 - side).wait_recv()

            for face, (inner, outer, _, _, side) in enumerate(FACES):
                here = jnp.concatenate([own_depth[n] for n in outer], axis=0)
                there = jnp.concatenate([tall(dhalo.at[side], n) for n in outer], axis=0)
                got = pick(here, oh[face, 0]) + pick(there, oh[face, 1])
                for i in range(2):
                    depth_out[face, i] = got[i * lm : (i + 1) * lm]
                    speed[face, i] = jnp.sqrt(
                        jnp.maximum(own_depth[inner[i]], depth_out[face, i])
                    )
        for side in range(2):

            @pl.when(has[side])
            def _():
                halo_copy(s, 1 - side).wait_recv()

        for face, (inner, outer, nx, ny, side) in enumerate(FACES):
            x = jnp.concatenate(
                [halo[s, side, SENT[side].index(n) * 3 + f] for n in outer for f in range(3)],
                axis=0,
            )
            far = near[face] + pick(x, oh[face, 1])
            for i in range(2):
                n = inner[i]
                fh, fu, fv = (far[(i * 3 + f) * lm : (i * 3 + f + 1) * lm] for f in range(3))
                sp, do = speed[face, i], depth_out[face, i]
                if nx:
                    rate[n][0] += nx * (hu[n] - do * fu) + sp * (fh - q[n][0])
                    rate[n][1] += nx * (q[n][0] - fh) + sp * (fu - q[n][1])
                    rate[n][2] += sp * (fv - q[n][2])
                else:
                    rate[n][0] += ny * (hv[n] - do * fv) + sp * (fh - q[n][0])
                    rate[n][1] += sp * (fu - q[n][1])
                    rate[n][2] += ny * (q[n][0] - fh) + sp * (fv - q[n][2])
        for n in range(4):
            for f in range(3):
                change = TIME_STEP * rate[n][f]
                if s:
                    change += SECTION_DECAY[s] * store[n * 3 + f]
                q[n][f] = q[n][f] + SECTION_GAIN[s] * change
                if s < 2:
                    store[n * 3 + f] = change
                    st[s + 1, n * 3 + f] = q[n][f]
                else:
                    fc[mm, n * 3 + f] = q[n][f]
        if s < 2:
            send_halo(s + 1)

    for f in range(3):
        em[mm, f] = 0.25 * ((q[0][f] + q[1][f]) + (q[2][f] + q[3][f]))

    def share(buf, send, recv, d):
        return pltpu.make_async_remote_copy(
            src_ref=buf.at[mm],
            dst_ref=buf.at[mm],
            send_sem=send.at[d],
            recv_sem=recv.at[d],
            device_id=mem_peers[d],
            device_id_type=MESH,
        )

    em_copies = [share(em, e_send, e_recv, d) for d in range(nm - 1)]
    fc_copies = [share(fc, f_send, f_recv, d) for d in range(nm - 1)]
    for copy in em_copies + fc_copies:
        copy.start()
    for copy in em_copies:
        copy.wait_recv()

    root = math.sqrt(members - 1)
    zs = [jnp.concatenate([em[j, f] for j in range(nm)], axis=0) for f in range(3)]
    zbar = [jnp.sum(z, axis=0, keepdims=True) * (1.0 / members) for z in zs]
    spread = [(z - b) * (1.0 / root) for z, b in zip(zs, zbar)]

    lanes = sums.shape[2]
    row = lax.broadcasted_iota(jnp.int32, (members, lanes), 0)
    lane = lax.broadcasted_iota(jnp.int32, (members, lanes), 1)
    eyes = jnp.where((lane == row) | (lane == row + members), 1.0, 0.0)
    w_row = w_col = None
    sum_copies = []
    for it in range(GN_ITERS):
        c = zbar
        if it:
            c = [
                b + jnp.sum(w_col * z, axis=0, keepdims=True) for b, z in zip(zbar, spread)
            ]
        hx = c[0] + c[1] * c[1] + c[2] * c[2]
        sens = (
            spread[0]
            + spread[1] * (2.0 * c[1] + spread[1])
            + spread[2] * (2.0 * c[2] + spread[2])
        )
        right = jnp.concatenate(
            [
                jnp.zeros((members, width), F32),
                sens * w2,
                jnp.broadcast_to(hx * w2 - wo, (8, width)),
                jnp.zeros((lanes - 2 * members - 8, width), F32),
            ],
            axis=0,
        )
        sums[it] = lax.dot_general(
            sens, right, (((1,), (1,)), ((), ())),
            precision=lax.Precision.HIGHEST, preferred_element_type=F32,
        )
        copies = [
            pltpu.make_async_remote_copy(
                src_ref=sums.at[it],
                dst_ref=parts.at[it, d],
                send_sem=s_send.at[it, d],
                recv_sem=s_recv.at[it, d],
                device_id=space_peers[d],
                device_id_type=MESH,
            )
            for d in range(ns - 1)
        ]
        for copy in copies:
            copy.start()
        total = sums[it]
        for d, copy in enumerate(copies):
            copy.wait_recv()
            total = total + parts[it, d]
        sum_copies += copies
        a = total + eyes
        if it:
            a = a + jnp.where(lane == 2 * members, w_col, 0.0)
        for k in range(members):
            pivot = a[k : k + 1, :]
            col = a[:, members + k : members + k + 1]
            inv = lax.rsqrt(a[k : k + 1, members + k : members + k + 1])
            pivot = pivot * inv
            a = jnp.where(row > k, a - (col * inv) * pivot, jnp.where(row == k, pivot, a))
        step = jnp.sum(a[:, 2 * members : 2 * members + 1] * a, axis=0, keepdims=True)
        w_row = -step if it == 0 else w_row - step
        w_col = jnp.sum(jnp.where(lane == row, w_row, 0.0), axis=1, keepdims=True)

    coef = jnp.where(lane < members, a + w_row * (1.0 / root), 0.0)
    mix = coef + 1.0 / members - jnp.sum(coef, axis=1, keepdims=True) * (1.0 / members)
    own = mix[0:lm]
    for j in range(1, nm):
        own = jnp.where(mm == j, mix[j * lm : (j + 1) * lm], own)
    gains = [jnp.broadcast_to(own[:, m : m + 1], (lm, width)) for m in range(members)]
    for copy in fc_copies:
        copy.wait_recv()
    for n in range(4):
        for f in range(3):
            acc = None
            for j in range(nm):
                block = fc[j, n * 3 + f]
                for i in range(lm):
                    term = gains[j * lm + i] * block[i : i + 1, :]
                    acc = term if acc is None else acc + term
            out_ref[:, f * 4 + n, :] = acc

    for side in range(2):

        @pl.when(has[side])
        def _():
            depth_copy(side).wait_send()
            for s in range(3):
                halo_copy(s, side).wait_send()

    for copy in em_copies + fc_copies + sum_copies:
        copy.wait_send()


def solution(mesh):
    nm, ns = mesh.shape["mem"], mesh.shape["space"]

    def body(states, depth, neighbours, obs_element, obs_count, obs_values, obs_error):
        lm, comps, width = states.shape
        slots = obs_values.shape[0]
        members = nm * lm
        lanes = -(-(2 * members + 8) // 128) * 128
        vmem = pl.BlockSpec(memory_space=pltpu.VMEM)
        dma = pltpu.SemaphoreType.DMA
        peers = max(nm - 1, 1)
        return pl.pallas_call(
            functools.partial(kernel, nm, ns),
            out_shape=jax.ShapeDtypeStruct(states.shape, F32),
            in_specs=[vmem] * 4 + [pl.BlockSpec(memory_space=pltpu.SMEM)] + [vmem] * 2,
            out_specs=vmem,
            scratch_shapes=[
                pltpu.VMEM((3, comps, lm, width), F32),
                pltpu.VMEM((comps, lm, width), F32),
                pltpu.VMEM((3, 2, 9, lm, width), F32),
                pltpu.VMEM((2, 4, width), F32),
                pltpu.VMEM((4, 2, width, width), BF16),
                pltpu.VMEM((nm, comps, lm, width), F32),
                pltpu.VMEM((nm, 3, lm, width), F32),
                pltpu.VMEM((GN_ITERS, ns - 1, members, lanes), F32),
                pltpu.VMEM((GN_ITERS, members, lanes), F32),
                dma((3, 2)),
                dma((3, 2)),
                dma((2,)),
                dma((2,)),
                dma((peers,)),
                dma((peers,)),
                dma((peers,)),
                dma((peers,)),
                dma((GN_ITERS, ns - 1)),
                dma((GN_ITERS, ns - 1)),
            ],
            compiler_params=pltpu.CompilerParams(
                collective_id=0, has_side_effects=True, vmem_limit_bytes=40 * 1024 * 1024
            ),
        )(
            states,
            depth,
            neighbours,
            obs_element.reshape(1, slots),
            obs_count,
            obs_values.reshape(1, slots),
            obs_error.reshape(1, slots),
        )

    placed = (
        P("mem", None, "space"),
        P(None, "space"),
        P(None, "space"),
        P("space"),
        P("space"),
        P("space"),
        P("space"),
    )
    return jax.shard_map(
        body, mesh=mesh, in_specs=placed, out_specs=P("mem", None, "space"), check_vma=False
    )
```

time: 286 us -> 36.2 us (0.13)
  blocking collectives: 113 us -> 0 us
  other arithmetic: 63.3 us -> 0 us
  local copies, waits for them, and re-layouts: 64.6 us -> 1.68 us
  Pallas kernels: 0 us -> 33.6 us
  starting transfers between devices: 32.8 us -> 0 us
  waiting for transfers between devices: 6.11 us -> 0 us
    psum x4 -> x0, blocking collectives: 105 us -> none  [the longest x2 87.7 us: body(): lax.psum((jnp.dot(regrouped, regrouped.T, precision=lax.Precision.HIGHEST...]
    gather x22 -> x0, local copies, waits for them, and re-layouts: 40.4 us -> none  [the longest x12 25.2 us: tendency(): jnp.take(padded, links[face], axis=-1).reshape(lead + (3, 4, width))]
    pallas_call x0 -> x1, Pallas kernels: none -> 33.6 us  [body(): pl.pallas_call(functools.partial(kernel, nm, ns), out_shape=jax.ShapeDtyp...]
    ppermute x8 -> x0, starting transfers between devices: 22.9 us -> none  [the longest x4 17.8 us: with_halo(): lax.ppermute(tail, axis, [(i, (i + 1) % count) for i in range(ends)])]
    mul x31 -> x0, other arithmetic: 15.4 us -> none  [the longest x21 14.5 us: normal_flux(): depth_part * (normal_x * state[..., 1, :, :] + normal_y * state[..., 2, :...]
    select_n x18 -> x0, other arithmetic: 14.4 us -> none  [the longest x12 14.3 us: tendency(): jnp.take(padded, links[face], axis=-1).reshape(lead + (3, 4, width))]
    all_to_all x3 -> x0, starting transfers between devices: 9.85 us -> none  [the longest x2 6.51 us: body(): lax.all_to_all(sens, 'mem', split_axis=1, concat_axis=0, tiled=True)]
    another operation x13 -> x0, other arithmetic: 8.08 us -> none  [the longest x6 4.31 us: solve_step(): lower = jnp.linalg.cholesky(hessian)]
  transfers between devices with their start and end apart: 11 -> 0, of which waited for: 2 -> 0; matrix products, arithmetic and copies ran while one was open for 8% -> 0% of each run, Pallas kernels for 0% -> 0%
where the time goes in v1:
time: 36.2 us; the launch traced here: 36 us
  Pallas kernels  33.6 us (93%)
  local copies, waits for them, and re-layouts  1.68 us (5%)
  between operations  0.74 us (2%)
    pallas_call x1, Pallas kernels, body(): pl.pallas_call(functools.partial(kernel, nm, ns), out_shape=jax.ShapeDtyp...  33.6 us
    unnamed x11, local copies, waits for them, and re-layouts  0.98 us

profile of v1, /device:TPU:0, one launch (start us, length us, event | category | flops | bytes accessed | tf_op | source)
XLA Modules:
  0.0 36.0 jit_solution(2840165003456855045)
XLA Ops:
  0.7 0.0 copy-start
  0.7 0.0 copy-start.1
  0.7 0.0 copy-start.2
  0.7 0.0 copy-start.3
  0.7 0.0 copy-start.4
  0.7 1.0 %copy.8.x_ref = f32[8,12,256]{2,1,0:T(8,128)S(1)} copy(f32[8,12,256]{2,0,1:T(8,128)} %param.7) | data formatting | bytes 196608 | tf_op args[0]
  1.7 0.0 copy-done
  1.7 0.0 copy-done.1
  1.7 0.0 copy-done.2
  1.7 0.0 copy-done.3
  1.7 0.0 copy-done.4
  1.7 33.6 %shard_map.73 = f32[8,12,256]{2,1,0:T(8,128)S(1)} custom-call(f32[8,12,256]{2,1,0:T(8,128)S(1)} %copy.8.x_ref, f32[4,256]{1,0:T(4,128)S(1)} %copy-done, s32[4,256]{1,0:T(4,128)S(1)} %copy-done.1, s32[1,1024]{1,0:T(1,128)S(1)} %bitcast.3, s32[1]{0:T(128)S(6)} %copy.10.cnt_ref, f32[1,1024]{1,0:T(1,128)S(1)} %bitcast.4, f32[1,1024]{1,0:T(1,128)S(1)} %bitcast.5), custom_call_target="tpu_custom_call" | custom-call | tf_op jit(solution)/shard_map/pallas_call | solution.py:334
  35.3 0.7 %copy.9 = f32[8,12,256]{2,0,1:T(8,128)} copy(f32[8,12,256]{2,1,0:T(8,128)S(1)} %shard_map.73) | data formatting | bytes 196608 | tf_op jit(solution)/shard_map/pallas_call | solution.py:334
Async XLA Ops:
  0.7 1.0 %copy-start = (f32[4,256]{1,0:T(4,128)S(1)}, f32[4,256]{1,0:T(4,128)}, u32[]{:S(2)}) copy-start(f32[4,256]{1,0:T(4,128)} %dep_ref.1) | copy-start | bytes 12292
  0.7 1.0 %copy-start.1 = (s32[4,256]{1,0:T(4,128)S(1)}, s32[4,256]{1,0:T(4,128)}, u32[]{:S(2)}) copy-start(s32[4,256]{1,0:T(4,128)} %nb_ref.1) | copy-start | bytes 12292
  0.7 1.0 %copy-start.2 = (s32[1024]{0:T(1024)S(1)}, s32[1024]{0:T(1024)}, u32[]{:S(2)}) copy-start(s32[1024]{0:T(1024)} %param.10) | copy-start | bytes 12292
  0.7 1.0 %copy-start.3 = (f32[1024]{0:T(1024)S(1)}, f32[1024]{0:T(1024)}, u32[]{:S(2)}) copy-start(f32[1024]{0:T(1024)} %param.12) | copy-start | bytes 12292
  0.7 1.0 %copy-start.4 = (f32[1024]{0:T(1024)S(1)}, f32[1024]{0:T(1024)}, u32[]{:S(2)}) copy-start(f32[1024]{0:T(1024)} %param.13) | copy-start | bytes 12292

commit v2 on v1

--- a/solution.py
+++ b/solution.py
@@ -38,26 +38,56 @@
     return y[:rows] + y[rows : 2 * rows] + y[2 * rows :]
 
 
+def pack(x, packed):
+    if not packed:
+        return x
+    half, lanes = x.shape[0] // 2, x.shape[1]
+    lane = lax.broadcasted_iota(jnp.int32, (half, lanes), 1)
+    return jnp.where(lane < lanes // 2, x[:half], pltpu.roll(x[half:], lanes // 2, 1))
+
+
+def unpack(x, packed):
+    if not packed:
+        return x
+    return jnp.concatenate([x, pltpu.roll(x, x.shape[1] // 2, 1)], axis=0)
+
+
 def kernel(
     nm, ns,
-    x_ref, dep_ref, nb_ref, oe_ref, cnt_ref, ov_ref, er_ref,
+    x_in, dep_in, nb_in, oe_in, cnt_ref, ov_in, er_in,
     out_ref,
+    dep_ref, nb_ref, oe_ref, ov_ref, er_ref,
     st, store, halo, dhalo, oh, fc, em, parts, sums,
-    h_send, h_recv, d_send, d_recv, e_send, e_recv, f_send, f_recv, s_send, s_recv,
+    l_sem, h_send, h_recv, d_send, d_recv, e_send, e_recv, f_send, f_recv, s_send, s_recv,
 ):
     mm, me = lax.axis_index("mem"), lax.axis_index("space")
-    lm, _, width = x_ref.shape
+    lm, width = x_in.shape[2:]
     members = nm * lm
-    space_peers = [(mm, lax.rem(me + d, ns)) for d in range(1, ns)]
+    loads = [
+        pltpu.make_async_copy(src, dst, l_sem.at[i])
+        for i, (src, dst) in enumerate(
+            [
+                (nb_in, nb_ref), (er_in, er_ref), (oe_in, oe_ref), (ov_in, ov_ref),
+                (x_in, st.at[0]), (dep_in, dep_ref),
+            ]
+        )
+    ]
+    for load in loads:
+        load.start()
+    inner = 2 if ns % 2 == 0 else 1
+    base = lax.div(me, inner) * inner
+    stages = [
+        [(mm, base + lax.rem(me - base + d, inner)) for d in range(1, inner)],
+        [(mm, lax.rem(me + d * inner, ns)) for d in range(1, ns // inner)],
+    ]
+    stages = [peers for peers in stages if peers]
+    space_peers = sum(stages, []) + [(mm, lax.rem(me + d, ns)) for d in (1, ns - 1)]
     mem_peers = [(lax.rem(mm + d, nm), me) for d in range(1, nm)]
 
     barrier = pltpu.get_barrier_semaphore()
     for peer in space_peers + mem_peers:
         pl.semaphore_signal(barrier, inc=1, device_id=peer, device_id_type=MESH)
 
-    for n in range(4):
-        for f in range(3):
-            st[0, n * 3 + f] = x_ref[:, f * 4 + n, :]
     has = (me > 0, me < ns - 1)
     for side in range(2):
 
@@ -70,10 +100,10 @@
     pl.semaphore_wait(barrier, len(space_peers) + len(mem_peers))
 
     def halo_copy(s, side):
-        first = SENT[1 - side][0] * 3
+        first = SENT[1 - side][0]
         target = (mm, lax.rem(me + (ns - 1 if side == 0 else 1), ns))
         return pltpu.make_async_remote_copy(
-            src_ref=st.at[s, pl.ds(first, 9)],
+            src_ref=(st.at[s] if s else x_in).at[:, pl.ds(first, 3)],
             dst_ref=halo.at[s, 1 - side],
             send_sem=h_send.at[s, 1 - side],
             recv_sem=h_recv.at[s, 1 - side],
@@ -84,7 +114,7 @@
     def depth_copy(side):
         target = (mm, lax.rem(me + (ns - 1 if side == 0 else 1), ns))
         return pltpu.make_async_remote_copy(
-            src_ref=dep_ref,
+            src_ref=dep_in,
             dst_ref=dhalo.at[1 - side],
             send_sem=d_send.at[1 - side],
             recv_sem=d_recv.at[1 - side],
@@ -107,6 +137,7 @@
 
     send_halo(0)
 
+    loads[0].wait()
     rows = lax.broadcasted_iota(jnp.int32, (width, width), 0)
     for face in range(4):
         side = FACES[face][4]
@@ -114,6 +145,8 @@
         oh[face, 0] = jnp.where(rows + width == link, 1.0, 0.0).astype(BF16)
         oh[face, 1] = jnp.where(rows + 2 * width * side == link, 1.0, 0.0).astype(BF16)
 
+    for load in loads[1:4]:
+        load.wait()
     slots = ov_ref.shape[1]
     slot = lax.broadcasted_iota(jnp.int32, (1, slots), 1)
     weight = jnp.where(slot < cnt_ref[0], 1.0, 0.0) / er_ref[...]
@@ -132,11 +165,13 @@
     def tall(ref, n):
         return jnp.broadcast_to(ref[n : n + 1, :], (lm, width))
 
+    for load in loads[4:]:
+        load.wait()
     own_depth = [tall(dep_ref, n) for n in range(4)]
     depth_out, speed = {}, {}
 
     for s in range(3):
-        q = [[st[s, n * 3 + f] for f in range(3)] for n in range(4)]
+        q = [[st[s, f, n] for f in range(3)] for n in range(4)]
         near = []
         for face, (_, outer, _, _, side) in enumerate(FACES):
             x = jnp.concatenate([q[n][f] for n in outer for f in range(3)], axis=0)
@@ -173,7 +208,7 @@
 
         for face, (inner, outer, nx, ny, side) in enumerate(FACES):
             x = jnp.concatenate(
-                [halo[s, side, SENT[side].index(n) * 3 + f] for n in outer for f in range(3)],
+                [halo[s, side, f, SENT[side].index(n)] for n in outer for f in range(3)],
                 axis=0,
             )
             far = near[face] + pick(x, oh[face, 1])
@@ -193,13 +228,13 @@
             for f in range(3):
                 change = TIME_STEP * rate[n][f]
                 if s:
-                    change += SECTION_DECAY[s] * store[n * 3 + f]
+                    change += SECTION_DECAY[s] * store[f, n]
                 q[n][f] = q[n][f] + SECTION_GAIN[s] * change
                 if s < 2:
-                    store[n * 3 + f] = change
-                    st[s + 1, n * 3 + f] = q[n][f]
+                    store[f, n] = change
+                    st[s + 1, f, n] = q[n][f]
                 else:
-                    fc[mm, n * 3 + f] = q[n][f]
+                    fc[mm, f, n] = q[n][f]
         if s < 2:
             send_halo(s + 1)
 
@@ -228,7 +263,8 @@
     zbar = [jnp.sum(z, axis=0, keepdims=True) * (1.0 / members) for z in zs]
     spread = [(z - b) * (1.0 / root) for z, b in zip(zs, zbar)]
 
-    lanes = sums.shape[2]
+    lanes = sums.shape[3]
+    packed = sums.shape[2] < members
     row = lax.broadcasted_iota(jnp.int32, (members, lanes), 0)
     lane = lax.broadcasted_iota(jnp.int32, (members, lanes), 1)
     eyes = jnp.where((lane == row) | (lane == row + members), 1.0, 0.0)
@@ -255,28 +291,33 @@
             ],
             axis=0,
         )
-        sums[it] = lax.dot_general(
+        total = lax.dot_general(
             sens, right, (((1,), (1,)), ((), ())),
             precision=lax.Precision.HIGHEST, preferred_element_type=F32,
         )
-        copies = [
-            pltpu.make_async_remote_copy(
-                src_ref=sums.at[it],
-                dst_ref=parts.at[it, d],
-                send_sem=s_send.at[it, d],
-                recv_sem=s_recv.at[it, d],
-                device_id=space_peers[d],
-                device_id_type=MESH,
-            )
-            for d in range(ns - 1)
-        ]
-        for copy in copies:
-            copy.start()
-        total = sums[it]
-        for d, copy in enumerate(copies):
-            copy.wait_recv()
-            total = total + parts[it, d]
-        sum_copies += copies
+        total = pack(total, packed)
+        slot_at = 0
+        for stage, peers in enumerate(stages):
+            sums[it, stage] = total
+            copies = [
+                pltpu.make_async_remote_copy(
+                    src_ref=sums.at[it, stage],
+                    dst_ref=parts.at[it, slot_at + d],
+                    send_sem=s_send.at[it, slot_at + d],
+                    recv_sem=s_recv.at[it, slot_at + d],
+                    device_id=peer,
+                    device_id_type=MESH,
+                )
+                for d, peer in enumerate(peers)
+            ]
+            for copy in copies:
+                copy.start()
+            for d, copy in enumerate(copies):
+                copy.wait_recv()
+                total = total + parts[it, slot_at + d]
+            slot_at += len(peers)
+            sum_copies += copies
+        total = unpack(total, packed)
         a = total + eyes
         if it:
             a = a + jnp.where(lane == 2 * members, w_col, 0.0)
@@ -302,11 +343,11 @@
         for f in range(3):
             acc = None
             for j in range(nm):
-                block = fc[j, n * 3 + f]
+                block = fc[j, f, n]
                 for i in range(lm):
                     term = gains[j * lm + i] * block[i : i + 1, :]
                     acc = term if acc is None else acc + term
-            out_ref[:, f * 4 + n, :] = acc
+            out_ref[f * 4 + n] = acc
 
     for side in range(2):
 
@@ -328,24 +369,33 @@
         slots = obs_values.shape[0]
         members = nm * lm
         lanes = -(-(2 * members + 8) // 128) * 128
+        packed = members % 16 == 0 and 4 * members + 2 <= lanes
+        rows = members // 2 if packed else members
         vmem = pl.BlockSpec(memory_space=pltpu.VMEM)
+        hbm = pl.BlockSpec(memory_space=pl.ANY)
         dma = pltpu.SemaphoreType.DMA
         peers = max(nm - 1, 1)
-        return pl.pallas_call(
+        mixed = pl.pallas_call(
             functools.partial(kernel, nm, ns),
-            out_shape=jax.ShapeDtypeStruct(states.shape, F32),
-            in_specs=[vmem] * 4 + [pl.BlockSpec(memory_space=pltpu.SMEM)] + [vmem] * 2,
+            out_shape=jax.ShapeDtypeStruct((comps, lm, width), F32),
+            in_specs=[hbm] * 4 + [pl.BlockSpec(memory_space=pltpu.SMEM)] + [hbm] * 2,
             out_specs=vmem,
             scratch_shapes=[
-                pltpu.VMEM((3, comps, lm, width), F32),
-                pltpu.VMEM((comps, lm, width), F32),
-                pltpu.VMEM((3, 2, 9, lm, width), F32),
+                pltpu.VMEM((4, width), F32),
+                pltpu.VMEM((4, width), jnp.int32),
+                pltpu.VMEM((1, slots), jnp.int32),
+                pltpu.VMEM((1, slots), F32),
+                pltpu.VMEM((1, slots), F32),
+                pltpu.VMEM((3, 3, 4, lm, width), F32),
+                pltpu.VMEM((3, 4, lm, width), F32),
+                pltpu.VMEM((3, 2, 3, 3, lm, width), F32),
                 pltpu.VMEM((2, 4, width), F32),
                 pltpu.VMEM((4, 2, width, width), BF16),
-                pltpu.VMEM((nm, comps, lm, width), F32),
+                pltpu.VMEM((nm, 3, 4, lm, width), F32),
                 pltpu.VMEM((nm, 3, lm, width), F32),
-                pltpu.VMEM((GN_ITERS, ns - 1, members, lanes), F32),
-                pltpu.VMEM((GN_ITERS, members, lanes), F32),
+                pltpu.VMEM((GN_ITERS, ns - 1, rows, lanes), F32),
+                pltpu.VMEM((GN_ITERS, 2, rows, lanes), F32),
+                dma((6,)),
                 dma((3, 2)),
                 dma((3, 2)),
                 dma((2,)),
@@ -358,10 +408,10 @@
                 dma((GN_ITERS, ns - 1)),
             ],
             compiler_params=pltpu.CompilerParams(
-                collective_id=0, has_side_effects=True, vmem_limit_bytes=40 * 1024 * 1024
+                collective_id=0, has_side_effects=True, vmem_limit_bytes=56 * 1024 * 1024
             ),
         )(
-            states,
+            states.transpose(1, 0, 2).reshape(3, comps // 3, lm, width),
             depth,
             neighbours,
             obs_element.reshape(1, slots),
@@ -369,6 +419,7 @@
             obs_values.reshape(1, slots),
             obs_error.reshape(1, slots),
         )
+        return mixed.transpose(1, 0, 2)
 
     placed = (
         P("mem", None, "space"),

time: 36.2 us -> 35.9 us (level)
    pallas_call x1 -> x0, local copies, waits for them, and re-layouts: 0.7 us -> none  [body(): pl.pallas_call(functools.partial(kernel, nm, ns), out_shape=jax.ShapeDtyp...]
    unnamed x11 -> x1, local copies, waits for them, and re-layouts: 0.98 us -> 1.54 us
where the time goes in v2:
time: 35.9 us; the launch traced here: 35.8 us
  Pallas kernels  33.6 us (94%)
  local copies, waits for them, and re-layouts  1.54 us (4%)
  between operations  0.66 us (2%)
    pallas_call x1, Pallas kernels, body(): pl.pallas_call(functools.partial(kernel, nm, ns), out_shape=jax.ShapeDtyp...  33.6 us
    unnamed x1, local copies, waits for them, and re-layouts  1.54 us

profile of v2, /device:TPU:0, one launch (start us, length us, event | category | flops | bytes accessed | tf_op | source)
XLA Modules:
  0.0 35.8 jit_solution(2754994662359578485)
XLA Ops:
  0.7 33.6 %shard_map.73 = f32[12,8,256]{2,1,0:T(8,128)} custom-call(f32[3,4,8,256]{3,2,1,0:T(8,128)} %bitcast.8, f32[4,256]{1,0:T(4,128)} %dep_in.1, s32[4,256]{1,0:T(4,128)} %nb_in.1, s32[1,1024]{1,0:T(1,128)} %bitcast.9, s32[1]{0:T(128)S(6)} %copy.9.cnt_ref, f32[1,1024]{1,0:T(1,128)} %bitcast.10, f32[1,1024]{1,0:T(1,128)} %bitcast.11), custom_call_target="tpu_custom_call" | custom-call | tf_op jit(solution)/shard_map/pallas_call | solution.py:378
  34.2 1.5 %copy.10 = f32[8,12,256]{2,0,1:T(8,128)} copy(f32[8,12,256]{2,0,1:T(8,128)} %bitcast.7) | data formatting | bytes 196608

commit v3 on v2

--- a/solution.py
+++ b/solution.py
@@ -54,26 +54,14 @@
 
 def kernel(
     nm, ns,
-    x_in, dep_in, nb_in, oe_in, cnt_ref, ov_in, er_in,
+    x_ref, dep_ref, nb_ref, oe_ref, cnt_ref, ov_ref, er_ref,
     out_ref,
-    dep_ref, nb_ref, oe_ref, ov_ref, er_ref,
     st, store, halo, dhalo, oh, fc, em, parts, sums,
-    l_sem, h_send, h_recv, d_send, d_recv, e_send, e_recv, f_send, f_recv, s_send, s_recv,
+    h_send, h_recv, d_send, d_recv, e_send, e_recv, f_send, f_recv, s_send, s_recv,
 ):
     mm, me = lax.axis_index("mem"), lax.axis_index("space")
-    lm, width = x_in.shape[2:]
+    lm, _, width = x_ref.shape
     members = nm * lm
-    loads = [
-        pltpu.make_async_copy(src, dst, l_sem.at[i])
-        for i, (src, dst) in enumerate(
-            [
-                (nb_in, nb_ref), (er_in, er_ref), (oe_in, oe_ref), (ov_in, ov_ref),
-                (x_in, st.at[0]), (dep_in, dep_ref),
-            ]
-        )
-    ]
-    for load in loads:
-        load.start()
     inner = 2 if ns % 2 == 0 else 1
     base = lax.div(me, inner) * inner
     stages = [
@@ -88,6 +76,9 @@
     for peer in space_peers + mem_peers:
         pl.semaphore_signal(barrier, inc=1, device_id=peer, device_id_type=MESH)
 
+    for n in range(4):
+        for f in range(3):
+            st[0, f, n] = x_ref[:, f * 4 + n, :]
     has = (me > 0, me < ns - 1)
     for side in range(2):
 
@@ -103,7 +94,7 @@
         first = SENT[1 - side][0]
         target = (mm, lax.rem(me + (ns - 1 if side == 0 else 1), ns))
         return pltpu.make_async_remote_copy(
-            src_ref=(st.at[s] if s else x_in).at[:, pl.ds(first, 3)],
+            src_ref=st.at[s, :, pl.ds(first, 3)],
             dst_ref=halo.at[s, 1 - side],
             send_sem=h_send.at[s, 1 - side],
             recv_sem=h_recv.at[s, 1 - side],
@@ -114,7 +105,7 @@
     def depth_copy(side):
         target = (mm, lax.rem(me + (ns - 1 if side == 0 else 1), ns))
         return pltpu.make_async_remote_copy(
-            src_ref=dep_in,
+            src_ref=dep_ref,
             dst_ref=dhalo.at[1 - side],
             send_sem=d_send.at[1 - side],
             recv_sem=d_recv.at[1 - side],
@@ -137,7 +128,6 @@
 
     send_halo(0)
 
-    loads[0].wait()
     rows = lax.broadcasted_iota(jnp.int32, (width, width), 0)
     for face in range(4):
         side = FACES[face][4]
@@ -145,8 +135,6 @@
         oh[face, 0] = jnp.where(rows + width == link, 1.0, 0.0).astype(BF16)
         oh[face, 1] = jnp.where(rows + 2 * width * side == link, 1.0, 0.0).astype(BF16)
 
-    for load in loads[1:4]:
-        load.wait()
     slots = ov_ref.shape[1]
     slot = lax.broadcasted_iota(jnp.int32, (1, slots), 1)
     weight = jnp.where(slot < cnt_ref[0], 1.0, 0.0) / er_ref[...]
@@ -165,8 +153,6 @@
     def tall(ref, n):
         return jnp.broadcast_to(ref[n : n + 1, :], (lm, width))
 
-    for load in loads[4:]:
-        load.wait()
     own_depth = [tall(dep_ref, n) for n in range(4)]
     depth_out, speed = {}, {}
 
@@ -324,9 +310,9 @@
         for k in range(members):
             pivot = a[k : k + 1, :]
             col = a[:, members + k : members + k + 1]
-            inv = lax.rsqrt(a[k : k + 1, members + k : members + k + 1])
-            pivot = pivot * inv
-            a = jnp.where(row > k, a - (col * inv) * pivot, jnp.where(row == k, pivot, a))
+            head = col[k : k + 1]
+            ratio = pivot * (1.0 / head)
+            a = jnp.where(row > k, a - col * ratio, jnp.where(row == k, pivot * lax.rsqrt(head), a))
         step = jnp.sum(a[:, 2 * members : 2 * members + 1] * a, axis=0, keepdims=True)
         w_row = -step if it == 0 else w_row - step
         w_col = jnp.sum(jnp.where(lane == row, w_row, 0.0), axis=1, keepdims=True)
@@ -372,20 +358,14 @@
         packed = members % 16 == 0 and 4 * members + 2 <= lanes
         rows = members // 2 if packed else members
         vmem = pl.BlockSpec(memory_space=pltpu.VMEM)
-        hbm = pl.BlockSpec(memory_space=pl.ANY)
         dma = pltpu.SemaphoreType.DMA
         peers = max(nm - 1, 1)
         mixed = pl.pallas_call(
             functools.partial(kernel, nm, ns),
             out_shape=jax.ShapeDtypeStruct((comps, lm, width), F32),
-            in_specs=[hbm] * 4 + [pl.BlockSpec(memory_space=pltpu.SMEM)] + [hbm] * 2,
+            in_specs=[vmem] * 4 + [pl.BlockSpec(memory_space=pltpu.SMEM)] + [vmem] * 2,
             out_specs=vmem,
             scratch_shapes=[
-                pltpu.VMEM((4, width), F32),
-                pltpu.VMEM((4, width), jnp.int32),
-                pltpu.VMEM((1, slots), jnp.int32),
-                pltpu.VMEM((1, slots), F32),
-                pltpu.VMEM((1, slots), F32),
                 pltpu.VMEM((3, 3, 4, lm, width), F32),
                 pltpu.VMEM((3, 4, lm, width), F32),
                 pltpu.VMEM((3, 2, 3, 3, lm, width), F32),
@@ -395,7 +375,6 @@
                 pltpu.VMEM((nm, 3, lm, width), F32),
                 pltpu.VMEM((GN_ITERS, ns - 1, rows, lanes), F32),
                 pltpu.VMEM((GN_ITERS, 2, rows, lanes), F32),
-                dma((6,)),
                 dma((3, 2)),
                 dma((3, 2)),
                 dma((2,)),
@@ -408,10 +387,10 @@
                 dma((GN_ITERS, ns - 1)),
             ],
             compiler_params=pltpu.CompilerParams(
-                collective_id=0, has_side_effects=True, vmem_limit_bytes=56 * 1024 * 1024
+                collective_id=0, has_side_effects=True, vmem_limit_bytes=40 * 1024 * 1024
             ),
         )(
-            states.transpose(1, 0, 2).reshape(3, comps // 3, lm, width),
+            states,
             depth,
             neighbours,
             obs_element.reshape(1, slots),

time: 35.9 us -> 35.2 us (0.981)
  Pallas kernels: 33.6 us -> 32.7 us
    pallas_call x1, Pallas kernels: 33.6 us -> 32.7 us  [body(): pl.pallas_call(functools.partial(kernel, nm, ns), out_shape=jax.ShapeDtyp...]
    unnamed x1 -> x12, local copies, waits for them, and re-layouts: 1.54 us -> 1.62 us
where the time goes in v3:
time: 35.2 us; the launch traced here: 35 us
  Pallas kernels  32.7 us (93%)
  local copies, waits for them, and re-layouts  1.62 us (5%)
  between operations  0.74 us (2%)
    pallas_call x1, Pallas kernels, body(): pl.pallas_call(functools.partial(kernel, nm, ns), out_shape=jax.ShapeDtyp...  32.7 us
    unnamed x12, local copies, waits for them, and re-layouts  1.62 us

profile of v3, /device:TPU:0, one launch (start us, length us, event | category | flops | bytes accessed | tf_op | source)
XLA Modules:
  0.0 35.0 jit_solution(14081628688363118955)
XLA Ops:
  0.7 0.0 copy-start
  0.7 0.0 copy-start.1
  0.7 0.0 copy-start.2
  0.7 0.0 copy-start.3
  0.7 0.0 copy-start.4
  0.7 1.0 %copy.8.x_ref = f32[8,12,256]{2,1,0:T(8,128)S(1)} copy(f32[8,12,256]{2,0,1:T(8,128)} %param.7) | data formatting | bytes 196608 | tf_op args[0]
  1.7 0.0 copy-done
  1.7 0.0 copy-done.1
  1.7 0.0 copy-done.2
  1.7 0.0 copy-done.3
  1.7 0.0 copy-done.4
  1.7 32.7 %shard_map.73 = f32[12,8,256]{2,1,0:T(8,128)S(1)} custom-call(f32[8,12,256]{2,1,0:T(8,128)S(1)} %copy.8.x_ref, f32[4,256]{1,0:T(4,128)S(1)} %copy-done, s32[4,256]{1,0:T(4,128)S(1)} %copy-done.1, s32[1,1024]{1,0:T(1,128)S(1)} %bitcast.5, s32[1]{0:T(128)S(6)} %copy.10.cnt_ref, f32[1,1024]{1,0:T(1,128)S(1)} %bitcast.6, f32[1,1024]{1,0:T(1,128)S(1)} %bitcast.7), custom_call_target="tpu_custom_call" | custom-call | tf_op jit(solution)/shard_map/pallas_call | solution.py:363
  34.4 0.6 %copy.11 = f32[8,12,256]{2,0,1:T(8,128)} copy(f32[8,12,256]{2,0,1:T(8,128)S(1)} %bitcast.4) | data formatting | bytes 196608
Async XLA Ops:
  0.7 1.0 %copy-start = (f32[4,256]{1,0:T(4,128)S(1)}, f32[4,256]{1,0:T(4,128)}, u32[]{:S(2)}) copy-start(f32[4,256]{1,0:T(4,128)} %dep_ref.1) | copy-start | bytes 12292
  0.7 1.0 %copy-start.1 = (s32[4,256]{1,0:T(4,128)S(1)}, s32[4,256]{1,0:T(4,128)}, u32[]{:S(2)}) copy-start(s32[4,256]{1,0:T(4,128)} %nb_ref.1) | copy-start | bytes 12292
  0.7 1.0 %copy-start.2 = (s32[1024]{0:T(1024)S(1)}, s32[1024]{0:T(1024)}, u32[]{:S(2)}) copy-start(s32[1024]{0:T(1024)} %param.10) | copy-start | bytes 12292
  0.7 1.0 %copy-start.3 = (f32[1024]{0:T(1024)S(1)}, f32[1024]{0:T(1024)}, u32[]{:S(2)}) copy-start(f32[1024]{0:T(1024)} %param.12) | copy-start | bytes 12292
  0.7 1.0 %copy-start.4 = (f32[1024]{0:T(1024)S(1)}, f32[1024]{0:T(1024)}, u32[]{:S(2)}) copy-start(f32[1024]{0:T(1024)} %param.13) | copy-start | bytes 12292

commit v4 on v3

--- a/solution.py
+++ b/solution.py
@@ -186,13 +186,16 @@
                     speed[face, i] = jnp.sqrt(
                         jnp.maximum(own_depth[inner[i]], depth_out[face, i])
                     )
-        for side in range(2):
-
-            @pl.when(has[side])
-            def _():
-                halo_copy(s, 1 - side).wait_recv()
-
-        for face, (inner, outer, nx, ny, side) in enumerate(FACES):
+        waited = set()
+        for face in (0, 2, 1, 3):
+            inner, outer, nx, ny, side = FACES[face]
+            if side not in waited:
+                waited.add(side)
+
+                @pl.when(has[side])
+                def _():
+                    halo_copy(s, 1 - side).wait_recv()
+
             x = jnp.concatenate(
                 [halo[s, side, f, SENT[side].index(n)] for n in outer for f in range(3)],
                 axis=0,

time: 35.2 us -> 35.2 us (level)
  no operation moved by 1% of the time
where the time goes in v4:
time: 35.2 us; the launch traced here: 35.1 us
  Pallas kernels  32.7 us (93%)
  local copies, waits for them, and re-layouts  1.62 us (5%)
  between operations  0.74 us (2%)
    pallas_call x1, Pallas kernels, body(): pl.pallas_call(functools.partial(kernel, nm, ns), out_shape=jax.ShapeDtyp...  32.7 us
    unnamed x12, local copies, waits for them, and re-layouts  1.62 us

profile of v4, /device:TPU:0, one launch (start us, length us, event | category | flops | bytes accessed | tf_op | source)
XLA Modules:
  0.0 35.1 jit_solution(15975911090861217395)
XLA Ops:
  0.7 0.0 copy-start
  0.7 0.0 copy-start.1
  0.7 0.0 copy-start.2
  0.7 0.0 copy-start.3
  0.7 0.0 copy-start.4
  0.7 1.0 %copy.8.x_ref = f32[8,12,256]{2,1,0:T(8,128)S(1)} copy(f32[8,12,256]{2,0,1:T(8,128)} %param.7) | data formatting | bytes 196608 | tf_op args[0]
  1.7 0.0 copy-done
  1.7 0.0 copy-done.1
  1.7 0.0 copy-done.2
  1.7 0.0 copy-done.3
  1.7 0.0 copy-done.4
  1.7 32.7 %shard_map.73 = f32[12,8,256]{2,1,0:T(8,128)S(1)} custom-call(f32[8,12,256]{2,1,0:T(8,128)S(1)} %copy.8.x_ref, f32[4,256]{1,0:T(4,128)S(1)} %copy-done, s32[4,256]{1,0:T(4,128)S(1)} %copy-done.1, s32[1,1024]{1,0:T(1,128)S(1)} %bitcast.5, s32[1]{0:T(128)S(6)} %copy.10.cnt_ref, f32[1,1024]{1,0:T(1,128)S(1)} %bitcast.6, f32[1,1024]{1,0:T(1,128)S(1)} %bitcast.7), custom_call_target="tpu_custom_call" | custom-call | tf_op jit(solution)/shard_map/pallas_call | solution.py:366
  34.4 0.6 %copy.11 = f32[8,12,256]{2,0,1:T(8,128)} copy(f32[8,12,256]{2,0,1:T(8,128)S(1)} %bitcast.4) | data formatting | bytes 196608
Async XLA Ops:
  0.7 1.0 %copy-start = (f32[4,256]{1,0:T(4,128)S(1)}, f32[4,256]{1,0:T(4,128)}, u32[]{:S(2)}) copy-start(f32[4,256]{1,0:T(4,128)} %dep_ref.1) | copy-start | bytes 12292
  0.7 1.0 %copy-start.1 = (s32[4,256]{1,0:T(4,128)S(1)}, s32[4,256]{1,0:T(4,128)}, u32[]{:S(2)}) copy-start(s32[4,256]{1,0:T(4,128)} %nb_ref.1) | copy-start | bytes 12292
  0.7 1.0 %copy-start.2 = (s32[1024]{0:T(1024)S(1)}, s32[1024]{0:T(1024)}, u32[]{:S(2)}) copy-start(s32[1024]{0:T(1024)} %param.10) | copy-start | bytes 12292
  0.7 1.0 %copy-start.3 = (f32[1024]{0:T(1024)S(1)}, f32[1024]{0:T(1024)}, u32[]{:S(2)}) copy-start(f32[1024]{0:T(1024)} %param.12) | copy-start | bytes 12292
  0.7 1.0 %copy-start.4 = (f32[1024]{0:T(1024)S(1)}, f32[1024]{0:T(1024)}, u32[]{:S(2)}) copy-start(f32[1024]{0:T(1024)} %param.13) | copy-start | bytes 12292
